TPU v7x, 256 devices: a whole 4x4x8 slice. The times are simulated.
256 devices in a mesh: seq: 32 (over z, y), dp: 8 (over x, core).
Axes of the slice: x: 4, y: 4, z: 8, core: 2. Of those that a mesh axis runs over, the one named last changes fastest.
Arguments:
- queries: bfloat16 [32768, 32, 128], P(('dp', 'seq')), parts along dimension 0, may hold values from -4.5 to 4.5
- keys: bfloat16 [32768, 32, 128], P(('dp', 'seq')), parts along dimension 0, may hold values from -4.5 to 4.5
- values: bfloat16 [32768, 32, 128], P(('dp', 'seq')), parts along dimension 0, may hold values from -6 to 6
- cotangent: bfloat16 [32768, 32, 128], P(('dp', 'seq')), parts along dimension 0, may hold values from -6 to 6
- clip_ids: int32 [32768], P(('dp', 'seq')), parts along dimension 0, may hold values from 0 to 15, never falling along the last dimension, each value on 1 to 512 neighbouring positions
- clip_step: int32 [128], P('dp'), parts along dimension 0, may hold values from 0 to 999
- clip_weight: float32 [128], P('dp'), parts along dimension 0, may hold values from 0.3 to 3
- step_gate: float32 [1000, 32, 128], P(None, 'seq'), may hold values from -6 to 6
Outputs:
- grad_queries: bfloat16 [32768, 32, 128], P(('dp', 'seq')), parts along dimension 0
- grad_keys: bfloat16 [32768, 32, 128], P(('dp', 'seq')), parts along dimension 0
- grad_values: bfloat16 [32768, 32, 128], P(('dp', 'seq')), parts along dimension 0
- grad_table: float32 [8000, 32, 128], P('dp', 'seq'), parts along dimension 0
There are 8 independent parts, one for each index of `dp`. A program takes and returns all parts, laid end to end along the dimension named above; an argument that names none is the same for every part. Nothing has to cross between parts.
Inputs may be any that keep to these rules, and one draw needn't show every extreme that they name: `clip_ids`: clip numbers never fall along the tokens; each clip holds 1 to 512 tokens, and some clip exactly 512.
All inputs are finite; a program needn't handle non-finite values.
Results may differ from a plain program's by a relative error of at most 0.038.
Values may be sent and summed in bfloat16 or wider, within the bound.
A program may use at most 64 MiB of HBM per device.

v0:
```python
import math

import jax
import jax.numpy as jnp
from jax import lax
from jax.sharding import PartitionSpec as P

MAXCLIP = 512
QBLOCK = 512


def attend_head(head_q, head_k, head_v, head_dout, token_ids):
    total = head_q.shape[0]
    width = min(QBLOCK + 2 * MAXCLIP, total)
    blocks = total // QBLOCK
    factor = 1.0 / math.sqrt(head_q.shape[1])
    zeros_f = jnp.zeros(head_q.shape, jnp.float32)
    zeros_b = jnp.zeros(head_q.shape, jnp.bfloat16)

    def one_block(block, carry):
        acc_keys, acc_values, out_dq, out_attn = carry
        row_start = (block * QBLOCK).astype(jnp.int32)
        ids_rows = lax.dynamic_slice_in_dim(token_ids, row_start, QBLOCK)
        begin = jnp.sum((token_ids < ids_rows[0]).astype(jnp.int32))
        begin = jnp.minimum(begin, total - width)
        rows_q = lax.dynamic_slice_in_dim(head_q, row_start, QBLOCK)
        rows_do = lax.dynamic_slice_in_dim(head_dout, row_start, QBLOCK)
        win_k = lax.dynamic_slice_in_dim(head_k, begin, width)
        win_v = lax.dynamic_slice_in_dim(head_v, begin, width)
        ids_win = lax.dynamic_slice_in_dim(token_ids, begin, width)
        scores = jnp.dot(rows_q, win_k.T, preferred_element_type=jnp.float32) * factor
        same_clip = ids_rows[:, None] == ids_win[None, :]
        scores = jnp.where(same_clip, scores, -1e30)
        row_max = jnp.max(scores, axis=1, keepdims=True)
        expo_terms = jnp.exp(scores - row_max)
        probs = expo_terms / jnp.sum(expo_terms, axis=1, keepdims=True)
        probs_b = probs.astype(jnp.bfloat16)
        attn_rows = jnp.dot(probs_b, win_v, preferred_element_type=jnp.float32).astype(jnp.bfloat16)
        d_probs = jnp.dot(rows_do, win_v.T, preferred_element_type=jnp.float32)
        delta = jnp.sum(
            rows_do.astype(jnp.float32) * attn_rows.astype(jnp.float32), axis=1, keepdims=True
        )
        d_scores = (probs * (d_probs - delta) * factor).astype(jnp.bfloat16)
        dq_rows = jnp.dot(d_scores, win_k, preferred_element_type=jnp.float32).astype(jnp.bfloat16)
        dk_part = jnp.dot(d_scores.T, rows_q, preferred_element_type=jnp.float32)
        dv_part = jnp.dot(probs_b.T, rows_do, preferred_element_type=jnp.float32)
        acc_keys = lax.dynamic_update_slice_in_dim(
            acc_keys, lax.dynamic_slice_in_dim(acc_keys, begin, width) + dk_part, begin, 0
        )
        acc_values = lax.dynamic_update_slice_in_dim(
            acc_values, lax.dynamic_slice_in_dim(acc_values, begin, width) + dv_part, begin, 0
        )
        out_dq = lax.dynamic_update_slice_in_dim(out_dq, dq_rows, row_start, 0)
        out_attn = lax.dynamic_update_slice_in_dim(out_attn, attn_rows, row_start, 0)
        return (acc_keys, acc_values, out_dq, out_attn)

    acc_keys, acc_values, out_dq, out_attn = lax.fori_loop(
        0, blocks, one_block, (zeros_f, zeros_f, zeros_b, zeros_b)
    )
    return (out_dq, acc_keys.astype(jnp.bfloat16), acc_values.astype(jnp.bfloat16), out_attn)


def on_device(queries, keys, values, cotangent, clip_ids, clip_step, clip_weight, step_gate):
    highest = lax.Precision.HIGHEST
    clip_count = clip_weight.shape[0]
    step_count = step_gate.shape[0]
    ids_all = lax.all_gather(clip_ids, "seq", axis=0, tiled=True)
    head_q, head_k, head_v, head_cot = (
        lax.all_to_all(queries, "seq", split_axis=1, concat_axis=0, tiled=True),
        lax.all_to_all(keys, "seq", split_axis=1, concat_axis=0, tiled=True),
        lax.all_to_all(values, "seq", split_axis=1, concat_axis=0, tiled=True),
        lax.all_to_all(cotangent, "seq", split_axis=1, concat_axis=0, tiled=True),
    )
    onehot_tok = (ids_all[:, None] == jnp.arange(clip_count, dtype=jnp.int32)[None, :]).astype(
        jnp.float32
    )
    onehot_step = (clip_step[:, None] == jnp.arange(step_count, dtype=jnp.int32)[None, :]).astype(
        jnp.float32
    )
    gate_clip = jnp.einsum("cn,nhe->che", onehot_step, step_gate, precision=highest)
    weighted = gate_clip * clip_weight[:, None, None]
    token_scale = jnp.einsum("tc,che->the", onehot_tok, weighted, precision=highest)
    head_dout = (token_scale * head_cot.astype(jnp.float32)).astype(jnp.bfloat16)
    results = [attend_head(head_q[:, 0], head_k[:, 0], head_v[:, 0], head_dout[:, 0], ids_all)]
    grad_q = jnp.stack([item[0] for item in results], axis=1)
    grad_k = jnp.stack([item[1] for item in results], axis=1)
    grad_v = jnp.stack([item[2] for item in results], axis=1)
    attn_out = jnp.stack([item[3] for item in results], axis=1)
    grad_q, grad_k, grad_v, attn_local = (
        lax.all_to_all(grad_q, "seq", split_axis=0, concat_axis=1, tiled=True),
        lax.all_to_all(grad_k, "seq", split_axis=0, concat_axis=1, tiled=True),
        lax.all_to_all(grad_v, "seq", split_axis=0, concat_axis=1, tiled=True),
        lax.all_to_all(attn_out, "seq", split_axis=0, concat_axis=1, tiled=True),
    )
    onehot_local = (clip_ids[:, None] == jnp.arange(clip_count, dtype=jnp.int32)[None, :]).astype(
        jnp.float32
    )
    local_weight = jnp.dot(onehot_local, clip_weight, precision=highest)
    terms = (
        local_weight[:, None, None] * cotangent.astype(jnp.float32) * attn_local.astype(jnp.float32)
    )
    partial_gate = jnp.einsum("tc,the->che", onehot_local, terms, precision=highest)
    grad_gate = lax.psum_scatter(partial_gate, "seq", scatter_dimension=1, tiled=True)
    grad_table = jnp.einsum("cn,che->nhe", onehot_step, grad_gate, precision=highest)
    return (grad_q, grad_k, grad_v, grad_table)


def solution(mesh):
    in_specs = (
        P(("dp", "seq"), None, None),
        P(("dp", "seq"), None, None),
        P(("dp", "seq"), None, None),
        P(("dp", "seq"), None, None),
        P(("dp", "seq")),
        P("dp"),
        P("dp"),
        P(None, "seq", None),
    )
    out_specs = (
        P(("dp", "seq"), None, None),
        P(("dp", "seq"), None, None),
        P(("dp", "seq"), None, None),
        P("dp", "seq", None),
    )
    return jax.shard_map(
        on_device, mesh=mesh, in_specs=in_specs, out_specs=out_specs, check_vma=False
    )
```

profile of v0, /device:TPU:6, one launch (start us, length us, event | category | flops | bytes accessed | tf_op | source)
XLA Modules:
  0.0 682.1 jit_solution(6129261826328806927)
XLA Ops:
  7.2 2.7 copy.63
  9.9 11.6 %all-to-all-start = ((bf16[128,32,128]{2,0,1:T(8,128)(2,1)}), bf16[128,32,128]{2,0,1:T(8,128)(2,1)}, u32[]{:S(2)}, u32[]{:S(2)}) async-start(bf16[128,32,128]{2,0,1:T(8,128)(2,1)} %copy.63), calls=%async_computation | async-start | bytes 2097152 | tf_op jit(solution)/shard_map/all_to_all | solution.py:69
  22.9 26.7 %all-to-all-done = bf16[128,32,128]{2,0,1:T(8,128)(2,1)} async-done(((bf16[128,32,128]{2,0,1:T(8,128)(2,1)}), bf16[128,32,128]{2,0,1:T(8,128)(2,1)}, u32[]{:S(2)}, u32[]{:S(2)}) %all-to-all-start) | async-done | bytes 1048608 | tf_op jit(solution)/shard_map/all_to_all | solution.py:69
  49.6 5.7 all-to-all-start.1
  56.7 25.6 %all-to-all-done.1 = bf16[128,32,128]{2,0,1:T(8,128)(2,1)} async-done(((bf16[128,32,128]{2,0,1:T(8,128)(2,1)}), bf16[128,32,128]{2,0,1:T(8,128)(2,1)}, u32[]{:S(2)}, u32[]{:S(2)}) %all-to-all-start.1) | async-done | bytes 1048608 | tf_op jit(solution)/shard_map/all_to_all | solution.py:70
  82.2 5.6 all-to-all-start.2
  89.3 25.1 %all-to-all-done.2 = bf16[128,32,128]{2,0,1:T(8,128)(2,1)S(1)} async-done(((bf16[128,32,128]{2,0,1:T(8,128)(2,1)}), bf16[128,32,128]{2,0,1:T(8,128)(2,1)S(1)}, u32[]{:S(2)}, u32[]{:S(2)}) %all-to-all-start.2) | async-done | bytes 1048608 | tf_op jit(solution)/shard_map/all_to_all | solution.py:72
  114.3 5.6 all-to-all-start.3
  120.0 55.1 %all-gather = s32[32,1,128]{2,1,0:T(1,128)S(1)} all-gather(s32[1,1,128]{2,1,0:T(1,128)S(1)} %bitcast.92), channel_id=1, replica_groups=mesh['seq'=32,'dp'=8] {'seq'}, dimensions={0}, use_global_device_ids=true | all-gather | bytes 16896 | tf_op jit(solution)/shard_map/all_gather | solution.py:67
  175.7 2.8 fusion.20
  183.6 169.7 %while.19 = (s32[]{:T(128)}, f32[4096,128]{1,0:T(8,128)}, f32[4096,128]{1,0:T(8,128)}, bf16[4096,128]{1,0:T(8,128)(2,1)}, bf16[4096,128]{0,1:T(8,128)(2,1)}, /*i...) while((s32[]{:T(128)}, f32[4096,128]{1,0:T(8,128)}, ...), condition=%wide.region_5.6_spmd, body=%wide.region_0.5_spmd.sunk | while | flops 1219766784 | bytes 36362548 | solution.py:57
  193.4 1.8 convolution_add_fusion.4
  195.2 2.2 fusion.65
  198.1 3.5 dynamic_update_slice.36
  201.6 3.5 dynamic_update_slice.37
  214.9 1.8 convolution_add_fusion.4
  216.7 2.2 fusion.65
  219.6 3.5 dynamic_update_slice.36
  223.1 3.5 dynamic_update_slice.37
  236.4 1.8 convolution_add_fusion.4
  238.2 2.2 fusion.65
  241.1 3.5 dynamic_update_slice.36
  244.6 3.5 dynamic_update_slice.37
  257.9 1.8 convolution_add_fusion.4
  259.7 2.2 fusion.65
  262.6 3.5 dynamic_update_slice.36
  266.1 3.5 dynamic_update_slice.37
  279.4 1.8 convolution_add_fusion.4
  281.2 2.2 fusion.65
  284.1 3.5 dynamic_update_slice.36
  287.6 3.5 dynamic_update_slice.37
  300.9 1.8 convolution_add_fusion.4
  302.8 2.2 fusion.65
  305.7 3.4 dynamic_update_slice.36
  309.1 3.4 dynamic_update_slice.37
  322.2 1.8 convolution_add_fusion.4
  324.0 2.2 fusion.65
  326.9 3.0 dynamic_update_slice.36
  329.9 3.0 dynamic_update_slice.37
  342.7 1.8 convolution_add_fusion.4
  344.5 2.2 fusion.65
  347.4 3.0 dynamic_update_slice.36
  350.4 3.0 dynamic_update_slice.37
  353.8 2.6 reduce.3
  358.3 5.8 all-to-all-start.7
  364.1 2.1 reduce
  366.2 2.3 reshape.59
  368.5 14.5 %all-to-all-done.7 = bf16[32,2,8192]{2,1,0:T(2,128)(2,1)} async-done(((bf16[32,2,8192]{2,1,0:T(2,128)(2,1)}), bf16[32,2,8192]{2,1,0:T(2,128)(2,1)}, u32[]{:S(2)}, u32[]{:S(2)}) %all-to-all-start.7) | async-done | bytes 1048608 | tf_op jit(solution)/shard_map/all_to_all | solution.py:93
  383.0 6.7 all-to-all-start.4
  389.7 3.4 convert_bitcast_fusion
  393.1 2.7 reduce.1
  396.9 13.1 %all-to-all-done.4 = bf16[32,2,8192]{2,1,0:T(2,128)(2,1)} async-done(((bf16[32,2,8192]{2,1,0:T(2,128)(2,1)}), bf16[32,2,8192]{2,1,0:T(2,128)(2,1)}, u32[]{:S(2)}, u32[]{:S(2)}) %all-to-all-start.4) | async-done | bytes 1048608 | tf_op jit(solution)/shard_map/all_to_all | solution.py:90
  410.0 7.7 %all-to-all-start.5 = ((bf16[32,2,8192]{2,1,0:T(2,128)(2,1)}), bf16[32,2,8192]{2,1,0:T(2,128)(2,1)S(1)}, u32[]{:S(2)}, u32[]{:S(2)}) async-start(bf16[32,2,8192]{2,1,0:T(2,128)(2,1)} %reshape.61), calls=%async_computation.5 | async-start | bytes 2097152 | tf_op jit(solution)/shard_map/all_to_all | solution.py:91
  417.7 2.7 reduce.2
  421.5 18.9 %all-to-all-done.5 = bf16[32,2,8192]{2,1,0:T(2,128)(2,1)S(1)} async-done(((bf16[32,2,8192]{2,1,0:T(2,128)(2,1)}), bf16[32,2,8192]{2,1,0:T(2,128)(2,1)S(1)}, u32[]{:S(2)}, u32[]{:S(2)}) %all-to-all-start.5) | async-done | bytes 1048608 | tf_op jit(solution)/shard_map/all_to_all | solution.py:91
  440.5 8.1 %all-to-all-start.6 = ((bf16[32,2,8192]{2,1,0:T(2,128)(2,1)}), bf16[32,2,8192]{2,1,0:T(2,128)(2,1)}, u32[]{:S(2)}, u32[]{:S(2)}) async-start(bf16[32,2,8192]{2,1,0:T(2,128)(2,1)} %reshape.63), calls=%async_computation.6 | async-start | bytes 2097152 | tf_op jit(solution)/shard_map/all_to_all | solution.py:92
  448.8 4.3 reshape.66
  453.1 2.2 convert_element_type.107
  456.6 2.7 fusion.21
  459.3 4.3 reshape.60
  465.4 4.3 reshape.62
  471.5 4.3 reshape.64
  477.7 195.4 %reduce-scatter.2.cloned.1.call-done = f32[16,1,128]{2,0,1:T(8,128)} async-done(((f32[16,32,128]{2,0,1:T(8,128)}), f32[16,1,128]{2,0,1:T(8,128)}) %reduce-scatter.2.cloned.1.call-update) | async-done | bytes 8208 | tf_op jit(solution)/shard_map/reduce_scatter | solution.py:103
  673.1 2.2 fusion.24
  (154 shorter events, 99.4 us)
Async XLA Ops:
  7.2 167.9 %copy-start = (f32[1000,1,128]{2,1,0:T(1,128)S(1)}, f32[1000,1,128]{2,1,0:T(1,128)}, u32[]{:S(2)}) copy-start(f32[1000,1,128]{2,1,0:T(1,128)} %param.17) | copy-start | bytes 1536004
  7.2 14.4 %copy-start.7 = (bf16[128,32,128]{2,1,0:T(8,128)(2,1)S(1)}, bf16[128,32,128]{2,1,0:T(8,128)(2,1)}, u32[]{:S(2)}) copy-start(bf16[128,32,128]{2,1,0:T(8,128)(2,1)} %param.11) | copy-start | bytes 3145732
  9.9 39.7 %all-to-all-start = ((bf16[128,32,128]{2,0,1:T(8,128)(2,1)}), bf16[128,32,128]{2,0,1:T(8,128)(2,1)}, u32[]{:S(2)}, u32[]{:S(2)}) async-start(bf16[128,32,128]{2,0,1:T(8,128)(2,1)} %copy.63), calls=%async_computation | async-start | bytes 2097152 | tf_op jit(solution)/shard_map/all_to_all | solution.py:69
  21.5 33.7 %copy-start.5 = (bf16[128,32,128]{2,1,0:T(8,128)(2,1)S(1)}, bf16[128,32,128]{2,1,0:T(8,128)(2,1)}, u32[]{:S(2)}) copy-start(bf16[128,32,128]{2,1,0:T(8,128)(2,1)} %param.13) | copy-start | bytes 3145732
  49.6 32.6 %all-to-all-start.1 = ((bf16[128,32,128]{2,0,1:T(8,128)(2,1)}), bf16[128,32,128]{2,0,1:T(8,128)(2,1)}, u32[]{:S(2)}, u32[]{:S(2)}) async-start(bf16[128,32,128]{2,0,1:T(8,128)(2,1)} %copy.64), calls=%async_computation.1 | async-start | bytes 2097152 | tf_op jit(solution)/shard_map/all_to_all | solution.py:70
  56.7 31.2 %copy-start.8 = (bf16[128,32,128]{2,1,0:T(8,128)(2,1)S(1)}, bf16[128,32,128]{2,1,0:T(8,128)(2,1)}, u32[]{:S(2)}) copy-start(bf16[128,32,128]{2,1,0:T(8,128)(2,1)} %param.12) | copy-start | bytes 3145732
  82.2 32.1 %all-to-all-start.2 = ((bf16[128,32,128]{2,0,1:T(8,128)(2,1)}), bf16[128,32,128]{2,0,1:T(8,128)(2,1)S(1)}, u32[]{:S(2)}, u32[]{:S(2)}) async-start(bf16[128,32,128]{2,0,1:T(8,128)(2,1)} %copy.65), calls=%async_computation.2 | async-start | bytes 2097152 | tf_op jit(solution)/shard_map/all_to_all | solution.py:72
  87.8 32.1 %copy-start.9 = (s32[128]{0:T(128)S(1)}, s32[128]{0:T(128)}, u32[]{:S(2)}) copy-start(s32[128]{0:T(128)} %param.14) | copy-start | bytes 1540
  87.9 87.3 %copy-start.10 = (s32[16]{0:T(128)S(1)}, s32[16]{0:T(128)}, u32[]{:S(2)}) copy-start(s32[16]{0:T(128)} %param.15) | copy-start | bytes 196
  87.9 87.2 %copy-start.11 = (f32[16]{0:T(128)S(1)}, f32[16]{0:T(128)}, u32[]{:S(2)}) copy-start(f32[16]{0:T(128)} %param.16) | copy-start | bytes 196
  114.3 64.1 %all-to-all-start.3 = ((bf16[128,32,128]{2,0,1:T(8,128)(2,1)}), bf16[128,32,128]{2,0,1:T(8,128)(2,1)S(1)}, u32[]{:S(2)}, u32[]{:S(2)}) async-start(bf16[128,32,128]{2,0,1:T(8,128)(2,1)} %copy.66), calls=%async_computation.3 | async-start | bytes 2097152 | tf_op jit(solution)/shard_map/all_to_all | solution.py:71
  357.2 7.0 %copy-start.4 = (bf16[4096,128]{1,0:T(8,128)(2,1)S(1)}, bf16[4096,128]{1,0:T(8,128)(2,1)}, u32[]{:S(2)}) copy-start(bf16[4096,128]{1,0:T(8,128)(2,1)} %get-tuple-element.176) | copy-start | bytes 3145732
  358.3 24.7 %all-to-all-start.7 = ((bf16[32,2,8192]{2,1,0:T(2,128)(2,1)}), bf16[32,2,8192]{2,1,0:T(2,128)(2,1)}, u32[]{:S(2)}, u32[]{:S(2)}) async-start(bf16[32,2,8192]{2,1,0:T(2,128)(2,1)} %reshape.65), calls=%async_computation.7 | async-start | bytes 2097152 | tf_op jit(solution)/shard_map/all_to_all | solution.py:93
  366.2 23.5 %copy-start.2 = (f32[4096,128]{1,0:T(8,128)S(1)}, f32[4096,128]{1,0:T(8,128)}, u32[]{:S(2)}) copy-start(f32[4096,128]{1,0:T(8,128)} %get-tuple-element.177) | copy-start | bytes 6291460
  383.0 27.1 %all-to-all-start.4 = ((bf16[32,2,8192]{2,1,0:T(2,128)(2,1)}), bf16[32,2,8192]{2,1,0:T(2,128)(2,1)}, u32[]{:S(2)}, u32[]{:S(2)}) async-start(bf16[32,2,8192]{2,1,0:T(2,128)(2,1)} %reshape.59), calls=%async_computation.4 | async-start | bytes 2097152 | tf_op jit(solution)/shard_map/all_to_all | solution.py:90
  410.0 30.4 %all-to-all-start.5 = ((bf16[32,2,8192]{2,1,0:T(2,128)(2,1)}), bf16[32,2,8192]{2,1,0:T(2,128)(2,1)S(1)}, u32[]{:S(2)}, u32[]{:S(2)}) async-start(bf16[32,2,8192]{2,1,0:T(2,128)(2,1)} %reshape.61), calls=%async_computation.5 | async-start | bytes 2097152 | tf_op jit(solution)/shard_map/all_to_all | solution.py:91
  440.5 8.2 %copy-start.3 = (bf16[32,2,8192]{2,1,0:T(2,128)(2,1)}, bf16[32,2,8192]{2,1,0:T(2,128)(2,1)S(1)}, u32[]{:S(2)}) copy-start(bf16[32,2,8192]{2,1,0:T(2,128)(2,1)S(1)} %all-to-all-done.5) | copy-start | bytes 3145732
  440.5 31.1 %all-to-all-start.6 = ((bf16[32,2,8192]{2,1,0:T(2,128)(2,1)}), bf16[32,2,8192]{2,1,0:T(2,128)(2,1)}, u32[]{:S(2)}, u32[]{:S(2)}) async-start(bf16[32,2,8192]{2,1,0:T(2,128)(2,1)} %reshape.63), calls=%async_computation.6 | async-start | bytes 2097152 | tf_op jit(solution)/shard_map/all_to_all | solution.py:92
  448.6 224.5 %reduce-scatter.2.cloned.1.call-start = ((), (), s32[]{:S(2)}) async-start(), calls=%async_computation.9 | async-start | bytes 270336 | tf_op jit(solution)/shard_map/reduce_scatter | solution.py:103
  453.1 2.2 copy-start.6
  475.8 199.4 %copy-start.1 = (f32[1000,1,128]{2,1,0:T(1,128)S(1)}, f32[1000,1,128]{2,1,0:T(1,128)}, u32[]{:S(2)}) copy-start(f32[1000,1,128]{2,1,0:T(1,128)} %param.17) | copy-start | bytes 1536004
Sparse Core Ops, SparseCore 0:
  459.4 213.5 reduce-scatter.1
where the time goes:
time: 686 us; the launch traced here: 682 us
  waiting for transfers between devices  319 us (47%)
  local copies, waits for them, and re-layouts  114 us (17%)
  matrix products  79.8 us (12%)
  starting transfers between devices  56.8 us (8%)
  blocking collectives  55.1 us (8%)
  other arithmetic  37.3 us (5%)
  between operations  14.3 us (2%)
    reduce_scatter x1, waiting for transfers between devices, on_device(): lax.psum_scatter(partial_gate, 'seq', scatter_dimension=1, tiled=True)  195 us
    all_gather x1, blocking collectives, on_device(): ids_all = lax.all_gather(clip_ids, 'seq', axis=0, tiled=True)  55.1 us
    unnamed x43, local copies, waits for them, and re-layouts  35.8 us
    dynamic_update_slice x8, local copies, waits for them, and re-layouts, one_block(): lax.dynamic_update_slice_in_dim(acc_keys, lax.dynamic_slice_in_dim(acc_ke...  26.8 us
    dynamic_update_slice x8, local copies, waits for them, and re-layouts, one_block(): lax.dynamic_update_slice_in_dim(acc_values, lax.dynamic_slice_in_dim(acc_...  26.8 us
    all_to_all x1, waiting for transfers between devices, on_device(): lax.all_to_all(queries, 'seq', split_axis=1, concat_axis=0, tiled=True)  26.7 us
    all_to_all x1, waiting for transfers between devices, on_device(): lax.all_to_all(keys, 'seq', split_axis=1, concat_axis=0, tiled=True)  25.6 us
    all_to_all x1, waiting for transfers between devices, on_device(): lax.all_to_all(cotangent, 'seq', split_axis=1, concat_axis=0, tiled=True)  25.1 us
  transfers between devices with their start and end apart: 9, of which 7 were waited for; matrix products, arithmetic and copies ran while one was open for 8% of the time, Pallas kernels for 0%

commit v1 on v0

v1 whole, which is shorter than its diff:
```python
import math

import jax
import jax.numpy as jnp
from jax import lax
from jax.experimental import pallas as pl
from jax.experimental.pallas import tpu as pltpu
from jax.sharding import PartitionSpec as P

NY = 4
NZ = 8
BLK = 128
ROW = NY * BLK
WIN = 2 * ROW
HD = 128
HEADS = 32
SLOTS = HEADS // NY
CLIPS = 16
STEPS = 1000
GRP = 16
QB = 256
AHEAD = 3
LAG_COMPUTE = 2
LAG_BACK = 5
MESH = pl.DeviceIdType.MESH
F32 = jnp.float32
BF16 = jnp.bfloat16


def nt(a, b):
    return lax.dot_general(a, b, (((1,), (1,)), ((), ())), preferred_element_type=F32)


def nn(a, b):
    return jnp.dot(a, b, preferred_element_type=F32)


def fill_clip_columns(idbuf, idcol):
    def one(b, _):
        line = idbuf[b, 0:1, :].astype(F32)
        idcol[pl.ds(pl.multiple_of(b * BLK, BLK), BLK), :] = jnp.broadcast_to(line, (BLK, BLK)).T
        return 0

    lax.fori_loop(0, 3 * NY, one, 0)


def attend(i, win, res, gate_in, idbuf, idcol, kt, vt, dout, acc):
    parity = lax.rem(i, 2)
    base = NY * (1 - parity)
    kt[...] = win[i, 1].T
    vt[...] = win[i, 2].T
    gate = gate_in[i]
    hi = gate.astype(BF16)
    rest = gate - hi.astype(F32)
    mid = rest.astype(BF16)
    low = (rest - mid.astype(F32)).astype(BF16)
    parts = jnp.concatenate([hi, mid, low, jnp.zeros((HD - 3 * CLIPS, HD), BF16)], axis=0)
    start = pl.multiple_of(base * BLK, BLK)
    lane = (lax.broadcasted_iota(jnp.int32, (WIN, HD), 1) % CLIPS).astype(F32)
    onehot = (idcol[pl.ds(start, WIN), :] == lane).astype(F32).astype(BF16)
    dout[...] = (nn(onehot, parts) * win[i, 3].astype(F32)).astype(BF16)
    acc[...] = jnp.zeros_like(acc)

    factor = 1.0 / math.sqrt(HD)
    not_mine = idcol[pl.ds(2 * ROW - ROW * (1 - parity) - (1 - parity), 1), :]
    edge = idcol[pl.ds(2 * ROW - ROW * parity - (1 - parity), 1), :]
    cid = lax.broadcasted_iota(jnp.int32, (CLIPS, QB), 0).astype(F32)
    per = QB // BLK

    def one(j, sums):
        at = pl.multiple_of(j * QB, QB)
        qb = win[i, 0, pl.ds(at, QB), :]
        db = dout[pl.ds(at, QB), :]
        ids_q = jnp.concatenate([idbuf[base + j * per + u, 0:1, :] for u in range(per)], axis=1)
        ids_q = ids_q.astype(F32)
        ids_k = idcol[pl.ds(start, WIN), :]
        same = jnp.concatenate([ids_k] * per, axis=1) == ids_q
        s = nt(win[i, 1], qb)
        s = jnp.where(same, s * (factor * math.log2(math.e)), -1e30)
        top = jnp.max(s, axis=0, keepdims=True)
        e = jnp.exp2(s - top)
        p = e * (1.0 / jnp.sum(e, axis=0, keepdims=True))
        pb = p.astype(BF16)
        o = nn(vt[...], pb).T.astype(BF16).astype(F32)
        dp = nt(win[i, 2], db)
        delta = jnp.sum((db.astype(F32) * o).T, axis=0, keepdims=True)
        ds = (p * (dp - delta) * factor).astype(BF16)
        res[i, 0, pl.ds(at, QB), :] = nn(kt[...], ds).T.astype(BF16)
        acc[0] += nn(ds, qb)
        acc[1] += nn(pb, db)
        nm = jnp.concatenate([not_mine] * per, axis=1)
        ed = jnp.concatenate([edge] * per, axis=1)
        halo = (j // (ROW // QB) + parity) % 2
        inside = jnp.full((1, QB), 1 - halo, jnp.int32).astype(F32)
        good = jnp.where(ids_q != nm, jnp.where(ids_q == ed, 1.0, inside), 0.0)
        pick = jnp.where(cid == ids_q, good, 0.0).astype(BF16)
        prod = win[i, 3, pl.ds(at, QB), :].astype(F32) * o
        ph = prod.astype(BF16)
        return sums + (nn(pick, ph) + nn(pick, (prod - ph.astype(F32)).astype(BF16)))

    sums = lax.fori_loop(0, WIN // QB, one, jnp.zeros((CLIPS, HD), F32))
    res[i, 1] = acc[0].astype(BF16)
    res[i, 2] = acc[1].astype(BF16)
    return sums


def kernel(
    step_ref, weight_ref, q_hbm, k_hbm, v_hbm, c_hbm, ids_ref, gate_ref,
    dq_ref, dk_ref, dv_ref, table_ref,
    stage, src, win, res, back, fin, idbuf, idcol, kt, vt, dout, acc, gate_in, sum_in, sum_out, wcol,
    perm, load_sem, own_sem,
    yin_s, yin_r, zin_s, zin_r, zout_s, zout_r, yout_s, yout_r, id_s, id_r, gate_s, gate_r, sum_s, sum_r,
):
    me = lax.axis_index("seq")
    z, y = me // NY, lax.rem(me, NY)

    def ypeer(d):
        return {"seq": z * NY + lax.rem(y + d, NY)}

    def zpeer(d):
        return {"seq": lax.rem(z + d, NZ) * NY + y}

    loads = [
        pltpu.make_async_copy(r, stage.at[a], load_sem.at[a])
        for a, r in enumerate((q_hbm, k_hbm, v_hbm, c_hbm))
    ]
    for c in loads:
        c.start()

    barrier = pltpu.get_barrier_semaphore()
    for d in range(1, NY):
        pl.semaphore_signal(barrier, inc=1, device_id=ypeer(d), device_id_type=MESH)
    for d in range(1, NZ):
        pl.semaphore_signal(barrier, inc=1, device_id=zpeer(d), device_id_type=MESH)

    row = lax.broadcasted_iota(jnp.int32, (GRP * GRP, GRP * GRP), 0)
    col = lax.broadcasted_iota(jnp.int32, (GRP * GRP, GRP * GRP), 1)
    perm[...] = (col == (row % GRP) * GRP + row // GRP).astype(F32).astype(BF16)
    for c in range(CLIPS):
        wcol[c : c + 1, :] = jnp.full((1, HD), weight_ref[c], F32)
        gate_in[z, c : c + 1, :] = gate_ref[pl.ds(step_ref[c], 1), :] * weight_ref[c]
    idbuf[NY + y] = jnp.broadcast_to(ids_ref[...], (8, BLK))
    for c in loads:
        c.wait()

    def lay_in(g):
        def one(n, _):
            a, t = n // (BLK // GRP), lax.rem(n, BLK // GRP)
            at = pl.ds(pl.multiple_of(t * GRP, GRP), GRP)
            x = stage[a, at, g * GRP : (g + 1) * GRP, :].reshape(GRP * GRP, HD)
            src[g * GRP : (g + 1) * GRP, a, at, :] = nn(perm[...], x).astype(BF16).reshape(GRP, GRP, HD)
            return 0

        lax.fori_loop(0, 4 * (BLK // GRP), one, 0)

    def lay_out(g):
        def one(t, _):
            at = pl.ds(pl.multiple_of(t * GRP, GRP), GRP)
            for a, out in enumerate((dq_ref, dk_ref, dv_ref)):
                x = fin[g * GRP : (g + 1) * GRP, a, at, :].reshape(GRP * GRP, HD)
                out[at, g * GRP : (g + 1) * GRP, :] = nn(perm[...], x).astype(BF16).reshape(GRP, GRP, HD)
            return 0

        lax.fori_loop(0, BLK // GRP, one, 0)

    def remote(s, d, ss, rs, to):
        return pltpu.make_async_remote_copy(
            src_ref=s, dst_ref=d, send_sem=ss, recv_sem=rs, device_id=to, device_id_type=MESH
        )

    def own_at(i):
        return pl.multiple_of(ROW * lax.rem(i, 2), ROW)

    def yin(i, d):
        to = ypeer(d)
        return remote(
            src.at[NY * i + lax.rem(y + d, NY)],
            win.at[i, :, pl.ds(pl.multiple_of(own_at(i) + y * BLK, BLK), BLK), :],
            yin_s.at[i, d - 1], yin_r.at[i, d - 1], to,
        )

    def own_copy(i):
        return pltpu.make_async_copy(
            src.at[NY * i + y],
            win.at[i, :, pl.ds(pl.multiple_of(own_at(i) + y * BLK, BLK), BLK), :],
            own_sem.at[i],
        )

    def zin(i):
        at = pl.ds(own_at(i), ROW)
        return remote(
            win.at[i, :, at, :], win.at[i, :, pl.ds(pl.multiple_of(ROW - own_at(i), ROW), ROW), :],
            zin_s.at[i], zin_r.at[i], zpeer(jnp.where(lax.rem(i, 2) == 0, NZ - 1, 1)),
        )

    def zout(i):
        at = pl.ds(pl.multiple_of(ROW - own_at(i), ROW), ROW)
        return remote(
            res.at[i, :, at, :], back.at[i],
            zout_s.at[i], zout_r.at[i], zpeer(jnp.where(lax.rem(i, 2) == 0, 1, NZ - 1)),
        )

    def yout(i, d):
        to = lax.rem(y + d, NY)
        return remote(
            res.at[i, :, pl.ds(pl.multiple_of(own_at(i) + to * BLK, BLK), BLK), :],
            fin.at[NY * i + y],
            yout_s.at[i, d - 1], yout_r.at[i, d - 1], ypeer(d),
        )

    def id_y(d):
        return remote(idbuf.at[NY + y], idbuf.at[NY + y], id_s.at[d - 1], id_r.at[d - 1], ypeer(d))

    def id_z(n):
        at = 0 if n == 0 else 2 * NY
        return remote(
            idbuf.at[pl.ds(NY, NY)], idbuf.at[pl.ds(at, NY)],
            id_s.at[NY - 1 + n], id_r.at[NY - 1 + n], zpeer(1 if n == 0 else NZ - 1),
        )

    def gate_copy(d):
        return remote(gate_in.at[z], gate_in.at[z], gate_s.at[d - 1], gate_r.at[d - 1], zpeer(d))

    def sum_copy(i):
        d = lax.rem(i - z + NZ, NZ)
        return remote(sum_out.at[i], sum_in.at[z], sum_s.at[i], sum_r.at[z], zpeer(d))

    lay_in(0)
    pl.semaphore_wait(barrier, NY - 1 + NZ - 1)

    for d in range(1, NY):
        id_y(d).start()
    for d in range(1, NZ):
        gate_copy(d).start()

    def begin(i):
        own_copy(i).start()
        for d in range(1, NY):
            yin(i, d).start()

    for i in range(AHEAD):
        begin(jnp.int32(i))
    lay_in(1)
    for d in range(1, NY):
        id_y(d).wait_recv()
    for n in range(2):
        id_z(n).start()
    for n in range(2):
        id_z(n).wait_recv()
    fill_clip_columns(idbuf, idcol)
    for d in range(1, NZ):
        gate_copy(d).wait_recv()

    def step(t, _):
        @pl.when(t < SLOTS)
        def _():
            own_copy(t).wait()
            for d in range(1, NY):
                yin(t, d).wait_recv()
            zin(t).start()

            @pl.when(t + AHEAD < SLOTS)
            def _():
                begin(t + AHEAD)

        @pl.when((t >= LAG_COMPUTE) & (t < SLOTS + LAG_COMPUTE))
        def _():
            i = t - LAG_COMPUTE
            zin(i).wait_recv()
            sums = attend(i, win, res, gate_in, idbuf, idcol, kt, vt, dout, acc)
            zout(i).start()
            sum_out[i] = sums * wcol[...]

            @pl.when(i != z)
            def _():
                sum_copy(i).start()

            @pl.when(i == z)
            def _():
                sum_in[z] = sum_out[i]

        @pl.when(t >= LAG_BACK)
        def _():
            i = t - LAG_BACK
            zout(i).wait_recv()
            parity = lax.rem(i, 2)
            other = idcol[pl.ds(2 * ROW - ROW * (1 - parity) - (1 - parity), 1), :]
            theirs = idcol[ROW : 2 * ROW, :] == other
            at = pl.ds(own_at(i), ROW)
            for a in range(3):
                res[i, a, at, :] = jnp.where(
                    theirs, back[i, a].astype(F32), res[i, a, at, :].astype(F32)
                ).astype(BF16)
            for d in range(1, NY):
                yout(i, d).start()
            fin[NY * i + y] = res[i, :, pl.ds(pl.multiple_of(own_at(i) + y * BLK, BLK), BLK), :]

        return 0

    lax.fori_loop(0, SLOTS + LAG_BACK, step, 0)

    def arrived(i, _):
        for d in range(1, NY):
            yout(i, d).wait_recv()
        return 0

    lax.fori_loop(0, SLOTS // 2, arrived, 0)
    lay_out(0)

    def sums_arrived(i, _):
        @pl.when(i != z)
        def _():
            remote(
                sum_out.at[i], sum_in.at[i], sum_s.at[i], sum_r.at[i], zpeer(lax.rem(i - z + NZ, NZ))
            ).wait_recv()

        return 0

    lax.fori_loop(0, NZ, sums_arrived, 0)
    total = sum_in[0]
    for r in range(1, NZ):
        total = total + sum_in[r]
    line = lax.broadcasted_iota(jnp.int32, (STEPS, HD), 0)
    table = jnp.zeros((STEPS, HD), F32)
    for c in range(CLIPS):
        table = table + jnp.where(line == step_ref[c], total[c : c + 1, :], 0.0)
    table_ref[...] = table

    lax.fori_loop(SLOTS // 2, SLOTS, arrived, 0)
    lay_out(1)

    def sent(i, _):
        for d in range(1, NY):
            yin(i, d).wait_send()
            yout(i, d).wait_send()
        zin(i).wait_send()
        zout(i).wait_send()

        @pl.when(i != z)
        def _():
            sum_copy(i).wait_send()

        return 0

    lax.fori_loop(0, SLOTS, sent, 0)
    for d in range(1, NY):
        id_y(d).wait_send()
    for n in range(2):
        id_z(n).wait_send()
    for d in range(1, NZ):
        gate_copy(d).wait_send()


def on_device(queries, keys, values, cotangent, clip_ids, clip_step, clip_weight, step_gate):
    vm = pl.BlockSpec(memory_space=pltpu.VMEM)
    sm = pl.BlockSpec(memory_space=pltpu.SMEM)
    hb = pl.BlockSpec(memory_space=pl.ANY)
    dma = pltpu.SemaphoreType.DMA
    grads = jax.ShapeDtypeStruct((BLK, HEADS, HD), BF16)
    dq, dk, dv, table = pl.pallas_call(
        kernel,
        out_shape=(grads, grads, grads, jax.ShapeDtypeStruct((STEPS, HD), F32)),
        in_specs=[sm, sm, hb, hb, hb, hb, vm, vm],
        out_specs=(vm, vm, vm, vm),
        scratch_shapes=[
            pltpu.VMEM((4, BLK, HEADS, HD), BF16),
            pltpu.VMEM((HEADS, 4, BLK, HD), BF16),
            pltpu.VMEM((SLOTS, 4, WIN, HD), BF16),
            pltpu.VMEM((SLOTS, 3, WIN, HD), BF16),
            pltpu.VMEM((SLOTS, 3, ROW, HD), BF16),
            pltpu.VMEM((HEADS, 3, BLK, HD), BF16),
            pltpu.VMEM((3 * NY, 8, BLK), jnp.int32),
            pltpu.VMEM((3 * ROW, BLK), F32),
            pltpu.VMEM((HD, WIN), BF16),
            pltpu.VMEM((HD, WIN), BF16),
            pltpu.VMEM((WIN, HD), BF16),
            pltpu.VMEM((2, WIN, HD), F32),
            pltpu.VMEM((NZ, CLIPS, HD), F32),
            pltpu.VMEM((NZ, CLIPS, HD), F32),
            pltpu.VMEM((NZ, CLIPS, HD), F32),
            pltpu.VMEM((CLIPS, HD), F32),
            pltpu.VMEM((GRP * GRP, GRP * GRP), BF16),
            dma((4,)), dma((SLOTS,)),
            dma((SLOTS, NY - 1)), dma((SLOTS, NY - 1)),
            dma((SLOTS,)), dma((SLOTS,)),
            dma((SLOTS,)), dma((SLOTS,)),
            dma((SLOTS, NY - 1)), dma((SLOTS, NY - 1)),
            dma((NY + 1,)), dma((NY + 1,)),
            dma((NZ - 1,)), dma((NZ - 1,)),
            dma((NZ,)), dma((NZ,)),
        ],
        compiler_params=pltpu.CompilerParams(
            collective_id=0, has_side_effects=True, vmem_limit_bytes=60 * 2**20
        ),
        cost_estimate=pl.CostEstimate(flops=12 * 2**30, bytes_accessed=8 * 2**20, transcendentals=2**23),
        name="clip_attention_backward",
    )(
        clip_step, clip_weight, queries, keys, values, cotangent,
        clip_ids.reshape(1, BLK), step_gate.reshape(STEPS, HD),
    )
    return dq, dk, dv, table.reshape(STEPS, 1, HD)


def solution(mesh):
    in_specs = (
        P(("dp", "seq"), None, None),
        P(("dp", "seq"), None, None),
        P(("dp", "seq"), None, None),
        P(("dp", "seq"), None, None),
        P(("dp", "seq")),
        P("dp"),
        P("dp"),
        P(None, "seq", None),
    )
    out_specs = (
        P(("dp", "seq"), None, None),
        P(("dp", "seq"), None, None),
        P(("dp", "seq"), None, None),
        P("dp", "seq", None),
    )
    return jax.shard_map(
        on_device, mesh=mesh, in_specs=in_specs, out_specs=out_specs, check_vma=False
    )
```

time: 686 us -> 143 us (0.21)
  waiting for transfers between devices: 319 us -> 0 us
  Pallas kernels: 0 us -> 136 us
  local copies, waits for them, and re-layouts: 114 us -> 6.11 us
  matrix products: 79.8 us -> 0 us
  starting transfers between devices: 56.8 us -> 0 us
  blocking collectives: 55.1 us -> 0 us
  other arithmetic: 37.3 us -> 0 us
  between operations: 14.3 us -> 0.65 us
    reduce_scatter x1 -> x0, waiting for transfers between devices: 195 us -> none  [on_device(): lax.psum_scatter(partial_gate, 'seq', scatter_dimension=1, tiled=True)]
    pallas_call x0 -> x1, Pallas kernels: none -> 136 us  [on_device(): pl.pallas_call(kernel, out_shape=(grads, grads, grads, jax.ShapeDtypeStru...]
    all_to_all x8 -> x0, waiting for transfers between devices: 124 us -> none  [the longest x1 26.7 us: on_device(): lax.all_to_all(queries, 'seq', split_axis=1, concat_axis=0, tiled=True)]
    dot_general x53 -> x0, matrix products: 79.8 us -> none  [the longest x8 17.9 us: one_block(): jnp.dot(d_scores, win_k, preferred_element_type=jnp.float32)]
    dynamic_update_slice x24 -> x0, local copies, waits for them, and re-layouts: 58.8 us -> none  [the longest x8 26.8 us: one_block(): lax.dynamic_update_slice_in_dim(acc_keys, lax.dynamic_slice_in_dim(acc_ke...]
    all_to_all x8 -> x0, starting transfers between devices: 56.8 us -> none  [the longest x1 11.6 us: on_device(): lax.all_to_all(queries, 'seq', split_axis=1, concat_axis=0, tiled=True)]
    all_gather x1 -> x0, blocking collectives: 55.1 us -> none  [on_device(): ids_all = lax.all_gather(clip_ids, 'seq', axis=0, tiled=True)]
    unnamed x43 -> x10, local copies, waits for them, and re-layouts: 35.8 us -> 6.11 us
  transfers between devices with their start and end apart: 9 -> 0, of which waited for: 7 -> 0; matrix products, arithmetic and copies ran while one was open for 8% -> 0% of each run, Pallas kernels for 0% -> 0%
where the time goes in v1:
time: 143 us
  Pallas kernels  136 us (95%)
  local copies, waits for them, and re-layouts  6.11 us (4%)
    pallas_call x1, Pallas kernels, on_device(): pl.pallas_call(kernel, out_shape=(grads, grads, grads, jax.ShapeDtypeStru...  136 us
    unnamed x10, local copies, waits for them, and re-layouts  6.11 us

profile of v1, /device:TPU:6, one launch (start us, length us, event | category | flops | bytes accessed | tf_op | source)
XLA Modules:
  0.0 142.9 jit_solution(8662728172572423321)
XLA Ops:
  0.6 136.2 %clip_attention_backward.1 = (bf16[128,32,128]{2,1,0:T(8,128)(2,1)}, bf16[128,32,128]{2,1,0:T(8,128)(2,1)}, bf16[128,32,128]{2,1,0:T(8,128)(2,1)}, f32[1000,128]{1,0:T(8,128)}) custom-call(s32[16]{0:T(128)} %step_ref.1, f32[16]{0:T(128)} %weight_ref.1, bf16[128,32,128]{2,1,0:T(8,128)(2,1)} %q_hbm.1, bf16[128,32,128]{2,1,0:T(8,128)(2,1)} %k_hbm.1, ...), custom_call_target="tpu_custom_call" | custom-call | flops 12884901888 | bytes 8388608 | tf_op jit(solution)/shard_map/clip_attention_backward/pallas_call | solution.py:360
  136.8 0.0 copy-start.1
  136.8 2.4 %copy.17 = bf16[128,32,128]{2,1,0:T(8,128)(2,1)} copy(bf16[128,32,128]{2,1,0:T(8,128)(2,1)} %get-tuple-element.20) | data formatting | bytes 2097152
  139.2 0.0 copy-done.1
  139.2 0.0 copy-start
  139.2 1.0 copy.18
  140.1 0.6 copy-done
  140.8 0.0 copy-start.2
  140.8 1.0 copy.19
  141.7 0.4 copy-done.2
  142.1 0.8 copy.20
Async XLA Ops:
  136.8 2.4 %copy-start.1 = (bf16[128,32,128]{2,1,0:T(8,128)(2,1)S(1)}, bf16[128,32,128]{2,1,0:T(8,128)(2,1)}, u32[]{:S(2)}) copy-start(bf16[128,32,128]{2,1,0:T(8,128)(2,1)} %get-tuple-element.21) | copy-start | bytes 3145732
  139.2 1.6 %copy-start = (bf16[128,32,128]{2,1,0:T(8,128)(2,1)S(1)}, bf16[128,32,128]{2,1,0:T(8,128)(2,1)}, u32[]{:S(2)}) copy-start(bf16[128,32,128]{2,1,0:T(8,128)(2,1)} %get-tuple-element.22) | copy-start | bytes 3145732
  140.8 1.4 copy-start.2

commit v2 on v1

v2 whole, which is shorter than its diff:
```python
import math

import jax
import jax.numpy as jnp
from jax import lax
from jax.experimental import pallas as pl
from jax.experimental.pallas import tpu as pltpu
from jax.sharding import PartitionSpec as P

NY = 4
NZ = 8
BLK = 128
ROW = NY * BLK
WIN = 2 * ROW
HD = 128
HEADS = 32
SLOTS = HEADS // NY
CLIPS = 16
STEPS = 1000
QB = 256
NEAR = 80.0
AHEAD = 3
LAG_COMPUTE = 3
LAG_BACK = 7
MESH = pl.DeviceIdType.MESH
F32 = jnp.float32
BF16 = jnp.bfloat16


def nt(a, b):
    return lax.dot_general(a, b, (((1,), (1,)), ((), ())), preferred_element_type=F32)


def nn(a, b):
    return jnp.dot(a, b, preferred_element_type=F32)


def fill_clips(idbuf, idcol, hot, near):
    lane = lax.broadcasted_iota(jnp.int32, (BLK, HD), 1)
    clip = (lane % CLIPS).astype(F32)
    once = jnp.where(lane < CLIPS, NEAR, 0.0)

    def one(b, _):
        at = pl.ds(pl.multiple_of(b * BLK, BLK), BLK)
        ids = jnp.broadcast_to(idbuf[b, 0:1, :].astype(F32), (BLK, BLK)).T
        idcol[at, :] = ids
        hot[at, :] = jnp.where(ids == clip, 1.0, 0.0).astype(BF16)
        near[at, :] = jnp.where(ids == clip, once, 0.0).astype(BF16)
        return 0

    lax.fori_loop(0, 3 * NY, one, 0)


def three_parts(x):
    hi = x.astype(BF16)
    rest = x - hi.astype(F32)
    mid = rest.astype(BF16)
    low = (rest - mid.astype(F32)).astype(BF16)
    return jnp.concatenate([hi, mid, low, jnp.zeros((HD - 3 * CLIPS, HD), BF16)], axis=0)


def other_clip(idcol, parity):
    return idcol[pl.ds(2 * ROW - (ROW + 1) * (1 - parity), 1), :]


def attend(i, win, res, gate_in, idbuf, idcol, hot, near, kt, vt, dout, probs, dscores):
    parity = lax.rem(i, 2)
    base = NY * (1 - parity)
    start = pl.multiple_of(base * BLK, BLK)
    kt[...] = win[i, 1].T
    vt[...] = win[i, 2].T
    scale = nn(hot[pl.ds(start, WIN), :], three_parts(gate_in[i]))
    dout[...] = (scale * win[i, 3].astype(F32)).astype(BF16)

    factor = 1.0 / math.sqrt(HD)
    per = QB // BLK
    not_mine = jnp.concatenate([other_clip(idcol, parity)] * per, axis=1)
    edge = jnp.concatenate([idcol[pl.ds(2 * ROW - ROW * parity - (1 - parity), 1), :]] * per, axis=1)
    cid = lax.broadcasted_iota(jnp.int32, (CLIPS, QB), 0).astype(F32)
    sums = jnp.zeros((CLIPS, HD), F32)
    for j in range(WIN // QB):
        lo, hi = max(0, j * QB - ROW), min(WIN, (j + 1) * QB + ROW)
        at = slice(j * QB, (j + 1) * QB)
        qb = win[i, 0, at, :]
        ids_q = jnp.concatenate([idbuf[base + j * per + u, 0:1, :] for u in range(per)], axis=1)
        ids_q = ids_q.astype(F32)
        near_k = near[pl.ds(pl.multiple_of(start + lo, QB), hi - lo), :]
        near_q = near[pl.ds(pl.multiple_of(start + j * QB, QB), QB), :]
        s = nt(jnp.concatenate([win[i, 1, lo:hi], near_k], axis=1), jnp.concatenate([qb, near_q], axis=1))
        top = jnp.max(s, axis=0, keepdims=True)
        e = jnp.exp2((s - top) * (factor * math.log2(math.e)))
        inv = 1.0 / jnp.sum(e, axis=0, keepdims=True)
        eb = e.astype(BF16)
        o = (nn(vt[:, lo:hi], eb) * inv).T.astype(BF16).astype(F32)
        db = (dout[at, :].astype(F32) * jnp.broadcast_to(inv, (HD, QB)).T).astype(BF16)
        dp = nt(win[i, 2, lo:hi], db)
        delta = jnp.sum((db.astype(F32) * o).T, axis=0, keepdims=True)
        ds = (e * (dp - delta)).astype(BF16)
        res[i, 0, at, :] = (nn(kt[:, lo:hi], ds) * factor).T.astype(BF16)
        probs[lo:hi, at] = eb
        dscores[lo:hi, at] = ds
        dout[at, :] = db
        halo = (j * QB // ROW + parity) % 2
        inside = jnp.full((1, QB), 1 - halo, jnp.int32).astype(F32)
        good = jnp.where(ids_q != not_mine, jnp.where(ids_q == edge, 1.0, inside), 0.0)
        pick = jnp.where(cid == ids_q, good, 0.0).astype(BF16)
        prod = win[i, 3, at, :].astype(F32) * o
        ph = prod.astype(BF16)
        sums = sums + (nn(pick, ph) + nn(pick, (prod - ph.astype(F32)).astype(BF16)))
    for k0, k1 in ((0, QB), (QB, WIN - QB), (WIN - QB, WIN)):
        q0, q1 = max(0, k0 - ROW), min(WIN, k1 + ROW)
        res[i, 1, k0:k1] = (nn(dscores[k0:k1, q0:q1], win[i, 0, q0:q1]) * factor).astype(BF16)
        res[i, 2, k0:k1] = nn(probs[k0:k1, q0:q1], dout[q0:q1]).astype(BF16)
    return sums


def kernel(
    step_ref, weight_ref, q_hbm, k_hbm, v_hbm, c_hbm, ids_ref, gate_hbm,
    fin_hbm, total_ref,
    stage, src, win, res, back, idbuf, idcol, hot, near, kt, vt, dout, probs, dscores,
    gates, gate_in, sum_in, sum_out, wcol,
    load_sem, own_sem, fin_sem,
    yin_s, yin_r, zin_s, zin_r, zout_s, zout_r, yout_s, yout_r, id_s, id_r, gate_s, gate_r, sum_s, sum_r,
):
    me = lax.axis_index("seq")
    z, y = me // NY, lax.rem(me, NY)

    def ypeer(d):
        return {"seq": z * NY + lax.rem(y + d, NY)}

    def zpeer(d):
        return {"seq": lax.rem(z + d, NZ) * NY + y}

    gate_load = pltpu.make_async_copy(gate_hbm, gates, load_sem.at[4])
    loads = [
        pltpu.make_async_copy(r, stage.at[a], load_sem.at[a])
        for a, r in enumerate((q_hbm, k_hbm, v_hbm, c_hbm))
    ]
    for c in loads:
        c.start()
    gate_load.start()

    barrier = pltpu.get_barrier_semaphore()
    for d in range(1, NY):
        pl.semaphore_signal(barrier, inc=1, device_id=ypeer(d), device_id_type=MESH)
    for d in range(1, NZ):
        pl.semaphore_signal(barrier, inc=1, device_id=zpeer(d), device_id_type=MESH)

    idbuf[NY + y] = jnp.broadcast_to(ids_ref[...], (8, BLK))
    for a, c in enumerate(loads):
        c.wait()
        src[:, a] = jnp.swapaxes(stage[a], 0, 1)

    def remote(s, d, ss, rs, to):
        return pltpu.make_async_remote_copy(
            src_ref=s, dst_ref=d, send_sem=ss, recv_sem=rs, device_id=to, device_id_type=MESH
        )

    def part(first, b):
        return pl.ds(pl.multiple_of(first + b * BLK, BLK), BLK)

    def own_at(i):
        return ROW * lax.rem(i, 2)

    def yin(i, d):
        return remote(
            src.at[NY * i + lax.rem(y + d, NY)], win.at[i, :, part(own_at(i), y), :],
            yin_s.at[i, d - 1], yin_r.at[i, d - 1], ypeer(d),
        )

    def own_copy(i):
        return pltpu.make_async_copy(
            src.at[NY * i + y], win.at[i, :, part(own_at(i), y), :], own_sem.at[i]
        )

    def zin_to(i):
        return zpeer(jnp.where(lax.rem(i, 2) == 0, NZ - 1, 1))

    def zin(i, b):
        return remote(
            win.at[i, :, part(own_at(i), b), :], win.at[i, :, part(ROW - own_at(i), b), :],
            zin_s.at[i, b], zin_r.at[i, b], zin_to(i),
        )

    def zin_own(i):
        return remote(
            src.at[NY * i + y], win.at[i, :, part(ROW - own_at(i), y), :],
            zin_s.at[i, y], zin_r.at[i, y], zin_to(i),
        )

    def zout(i, b):
        return remote(
            res.at[i, :, part(ROW - own_at(i), b), :], back.at[i, :, part(0, b), :],
            zout_s.at[i, b], zout_r.at[i, b], zpeer(jnp.where(lax.rem(i, 2) == 0, 1, NZ - 1)),
        )

    def yout(i, d):
        return remote(
            res.at[i, :, part(own_at(i), lax.rem(y + d, NY)), :], fin_hbm.at[NY * i + y],
            yout_s.at[i, d - 1], yout_r.at[i, d - 1], ypeer(d),
        )

    def fin_own(i):
        return pltpu.make_async_copy(
            res.at[i, :, part(own_at(i), y), :], fin_hbm.at[NY * i + y], fin_sem.at[i]
        )

    def id_y(d):
        return remote(idbuf.at[NY + y], idbuf.at[NY + y], id_s.at[d - 1], id_r.at[d - 1], ypeer(d))

    def id_z(n):
        return remote(
            idbuf.at[pl.ds(NY, NY)], idbuf.at[pl.ds(2 * NY * n, NY)],
            id_s.at[NY - 1 + n], id_r.at[NY - 1 + n], zpeer(1 if n == 0 else NZ - 1),
        )

    def gate_copy(d):
        return remote(gate_in.at[z], gate_in.at[z], gate_s.at[d - 1], gate_r.at[d - 1], zpeer(d))

    def sum_copy(i, slot):
        return remote(
            sum_out.at[i], sum_in.at[slot], sum_s.at[i], sum_r.at[slot], zpeer(lax.rem(i - z + NZ, NZ))
        )

    def begin(i):
        for d in range(1, NY):
            yin(i, d).start()
        own_copy(i).start()

    pl.semaphore_wait(barrier, NY - 1 + NZ - 1)
    for d in range(1, NY):
        id_y(d).start()
    begin(jnp.int32(0))

    def early(i, _):
        zin_own(i).start()
        return 0

    lax.fori_loop(0, SLOTS, early, 0)
    for i in range(1, AHEAD):
        begin(jnp.int32(i))
    gate_load.wait()
    for c in range(CLIPS):
        wcol[c : c + 1, :] = jnp.full((1, HD), weight_ref[c], F32)
        gate_in[z, c : c + 1, :] = gates[pl.ds(step_ref[c], 1), :] * weight_ref[c]
    for d in range(1, NZ):
        gate_copy(d).start()
    for d in range(1, NY):
        id_y(d).wait_recv()
    for n in range(2):
        id_z(n).start()

    def step(t, _):
        @pl.when(t < SLOTS)
        def _():
            for d in range(1, NY):
                yin(t, d).wait_recv()
                zin(t, lax.rem(y + NY - d, NY)).start()
            own_copy(t).wait()

            @pl.when(t + AHEAD < SLOTS)
            def _():
                begin(t + AHEAD)

        @pl.when(t == LAG_COMPUTE)
        def _():
            for n in range(2):
                id_z(n).wait_recv()
            fill_clips(idbuf, idcol, hot, near)
            for d in range(1, NZ):
                gate_copy(d).wait_recv()

        @pl.when((t >= LAG_COMPUTE) & (t < SLOTS + LAG_COMPUTE))
        def _():
            i = t - LAG_COMPUTE
            for b in range(NY):
                zin(i, b).wait_recv()
            sums = attend(
                i, win, res, gate_in, idbuf, idcol, hot, near, kt, vt, dout, probs, dscores
            )
            for d in (1, 2, 3, 0):
                zout(i, lax.rem(y + d, NY)).start()
            sum_out[i] = sums * wcol[...]

            @pl.when(i != z)
            def _():
                sum_copy(i, z).start()

            @pl.when(i == z)
            def _():
                sum_in[z] = sum_out[i]

        @pl.when((t >= LAG_BACK) & (lax.rem(t - LAG_BACK, 2) == 0))
        def _():
            for d in (1, 2, 3, 0):
                b = lax.rem(y + d, NY)
                for odd in range(2):
                    i = t - LAG_BACK + odd
                    zout(i, b).wait_recv()
                    theirs = idcol[part(ROW, b), :] == other_clip(idcol, odd)
                    for a in range(3):
                        res[i, a, part(ROW * odd, b), :] = jnp.where(
                            theirs,
                            back[i, a, part(0, b), :].astype(F32),
                            res[i, a, part(ROW * odd, b), :].astype(F32),
                        ).astype(BF16)
                    if d:
                        yout(i, d).start()
                    else:
                        fin_own(i).start()

        return 0

    lax.fori_loop(0, SLOTS + LAG_BACK - 1, step, 0)

    def sums_arrived(i, _):
        @pl.when(i != z)
        def _():
            sum_copy(i, i).wait_recv()

        return 0

    lax.fori_loop(0, NZ, sums_arrived, 0)
    total = sum_in[0]
    for r in range(1, NZ):
        total = total + sum_in[r]
    total_ref[...] = total

    def done(i, _):
        for d in range(1, NY):
            yin(i, d).wait_send()
            yout(i, d).wait_send()
            yout(i, d).wait_recv()
        for b in range(NY):
            zin(i, b).wait_send()
            zout(i, b).wait_send()
        fin_own(i).wait()

        @pl.when(i != z)
        def _():
            sum_copy(i, z).wait_send()

        return 0

    lax.fori_loop(0, SLOTS, done, 0)
    for d in range(1, NY):
        id_y(d).wait_send()
    for n in range(2):
        id_z(n).wait_send()
    for d in range(1, NZ):
        gate_copy(d).wait_send()


def lay_out(step_ref, total_ref, fin_hbm, dq_hbm, dk_hbm, dv_hbm, table_hbm, got, put, table, in_sem, out_sem):
    half = BLK // 2
    pieces = [(a, n) for a in range(3) for n in range(2)]
    ins = [
        pltpu.make_async_copy(
            fin_hbm.at[:, a, n * half : (n + 1) * half, :], got.at[a, n], in_sem.at[a, n]
        )
        for a, n in pieces
    ]
    outs = [
        pltpu.make_async_copy(
            put.at[a, n], (dq_hbm, dk_hbm, dv_hbm)[a].at[n * half : (n + 1) * half], out_sem.at[a, n]
        )
        for a, n in pieces
    ]
    for c in ins:
        c.start()
    lane = lax.broadcasted_iota(jnp.int32, (1, HD), 1) % CLIPS
    steps = jnp.zeros((1, HD), jnp.int32)
    for c in range(CLIPS):
        steps = jnp.where(lane == c, step_ref[c], steps)
    line = lax.broadcasted_iota(jnp.int32, (STEPS, HD), 0)
    pick = jnp.where(line == steps, 1.0, 0.0).astype(BF16)
    table[...] = nn(pick, three_parts(total_ref[...]))
    table_out = pltpu.make_async_copy(table, table_hbm, out_sem.at[3, 0])
    table_out.start()
    for (a, n), i, o in zip(pieces, ins, outs):
        i.wait()
        put[a, n] = jnp.swapaxes(got[a, n], 0, 1)
        o.start()
    for o in outs:
        o.wait()
    table_out.wait()


def on_device(queries, keys, values, cotangent, clip_ids, clip_step, clip_weight, step_gate):
    vm = pl.BlockSpec(memory_space=pltpu.VMEM)
    sm = pl.BlockSpec(memory_space=pltpu.SMEM)
    hb = pl.BlockSpec(memory_space=pl.ANY)
    dma = pltpu.SemaphoreType.DMA
    fin, total = pl.pallas_call(
        kernel,
        out_shape=(
            jax.ShapeDtypeStruct((HEADS, 3, BLK, HD), BF16),
            jax.ShapeDtypeStruct((CLIPS, HD), F32),
        ),
        in_specs=[sm, sm, hb, hb, hb, hb, vm, hb],
        out_specs=(hb, vm),
        scratch_shapes=[
            pltpu.VMEM((4, BLK, HEADS, HD), BF16),
            pltpu.VMEM((HEADS, 4, BLK, HD), BF16),
            pltpu.VMEM((SLOTS, 4, WIN, HD), BF16),
            pltpu.VMEM((SLOTS, 3, WIN, HD), BF16),
            pltpu.VMEM((SLOTS, 3, ROW, HD), BF16),
            pltpu.VMEM((3 * NY, 8, BLK), jnp.int32),
            pltpu.VMEM((3 * ROW, BLK), F32),
            pltpu.VMEM((3 * ROW, HD), BF16),
            pltpu.VMEM((3 * ROW, HD), BF16),
            pltpu.VMEM((HD, WIN), BF16),
            pltpu.VMEM((HD, WIN), BF16),
            pltpu.VMEM((WIN, HD), BF16),
            pltpu.VMEM((WIN, WIN), BF16),
            pltpu.VMEM((WIN, WIN), BF16),
            pltpu.VMEM((STEPS, HD), F32),
            pltpu.VMEM((NZ, CLIPS, HD), F32),
            pltpu.VMEM((NZ, CLIPS, HD), F32),
            pltpu.VMEM((NZ, CLIPS, HD), F32),
            pltpu.VMEM((CLIPS, HD), F32),
            dma((5,)), dma((SLOTS,)), dma((SLOTS,)),
            dma((SLOTS, NY - 1)), dma((SLOTS, NY - 1)),
            dma((SLOTS, NY)), dma((SLOTS, NY)),
            dma((SLOTS, NY)), dma((SLOTS, NY)),
            dma((SLOTS, NY - 1)), dma((SLOTS, NY - 1)),
            dma((NY + 1,)), dma((NY + 1,)),
            dma((NZ - 1,)), dma((NZ - 1,)),
            dma((NZ,)), dma((NZ,)),
        ],
        compiler_params=pltpu.CompilerParams(
            collective_id=0, has_side_effects=True, vmem_limit_bytes=60 * 2**20
        ),
        cost_estimate=pl.CostEstimate(flops=12 * 2**30, bytes_accessed=8 * 2**20, transcendentals=2**23),
        name="clip_attention_backward",
    )(
        clip_step, clip_weight, queries, keys, values, cotangent,
        clip_ids.reshape(1, BLK), step_gate.reshape(STEPS, HD),
    )
    grads = jax.ShapeDtypeStruct((BLK, HEADS, HD), BF16)
    dq, dk, dv, table = pl.pallas_call(
        lay_out,
        out_shape=(grads, grads, grads, jax.ShapeDtypeStruct((STEPS, HD), F32)),
        in_specs=[sm, vm, hb],
        out_specs=(hb, hb, hb, hb),
        scratch_shapes=[
            pltpu.VMEM((3, 2, HEADS, BLK // 2, HD), BF16),
            pltpu.VMEM((3, 2, BLK // 2, HEADS, HD), BF16),
            pltpu.VMEM((STEPS, HD), F32),
            dma((3, 2)), dma((4, 2)),
        ],
        compiler_params=pltpu.CompilerParams(vmem_limit_bytes=60 * 2**20),
        cost_estimate=pl.CostEstimate(flops=2**25, bytes_accessed=7 * 2**20, transcendentals=0),
        name="lay_out",
    )(clip_step, total, fin)
    return dq, dk, dv, table.reshape(STEPS, 1, HD)


def solution(mesh):
    in_specs = (
        P(("dp", "seq"), None, None),
        P(("dp", "seq"), None, None),
        P(("dp", "seq"), None, None),
        P(("dp", "seq"), None, None),
        P(("dp", "seq")),
        P("dp"),
        P("dp"),
        P(None, "seq", None),
    )
    out_specs = (
        P(("dp", "seq"), None, None),
        P(("dp", "seq"), None, None),
        P(("dp", "seq"), None, None),
        P("dp", "seq", None),
    )
    return jax.shard_map(
        on_device, mesh=mesh, in_specs=in_specs, out_specs=out_specs, check_vma=False
    )
```

time: 143 us -> 109 us (0.76)
  Pallas kernels: 136 us -> 108 us
  local copies, waits for them, and re-layouts: 6.11 us -> 0 us
    pallas_call x1 -> x2, Pallas kernels: 136 us -> 108 us  [the longest x1 104 us: on_device(): pl.pallas_call(kernel, out_shape=(jax.ShapeDtypeStruct((HEADS, 3, BLK, HD...]
    unnamed x10 -> x0, local copies, waits for them, and re-layouts: 6.11 us -> none
where the time goes in v2:
time: 109 us
  Pallas kernels  108 us (99%)
    pallas_call x1, Pallas kernels, on_device(): pl.pallas_call(kernel, out_shape=(jax.ShapeDtypeStruct((HEADS, 3, BLK, HD...  104 us
    pallas_call x1, Pallas kernels, on_device(): pl.pallas_call(lay_out, out_shape=(grads, grads, grads, jax.ShapeDtypeStr...  3.87 us

profile of v2, /device:TPU:6, one launch (start us, length us, event | category | flops | bytes accessed | tf_op | source)
XLA Modules:
  0.0 108.9 jit_solution(12447654845102624084)
XLA Ops:
  0.6 104.4 %clip_attention_backward.1 = (bf16[32,3,128,128]{3,2,1,0:T(8,128)(2,1)}, f32[16,128]{1,0:T(8,128)}) custom-call(s32[16]{0:T(128)} %step_ref.3, f32[16]{0:T(128)} %weight_ref.1, bf16[128,32,128]{2,1,0:T(8,128)(2,1)} %q_hbm.1, bf16[128,32,128]{2,1,0:T(8,128)(2,1)} %k_hbm.1, bf16[128,32,128]{2,1,0:T(8,128)(2,1)} %v_hbm.1, bf16[128,32,128]{2,1,0:T(8,128)(2,1)} %c_hbm.1, ...), custom_call_target="tpu_custom_call" | custom-call | flops 12884901888 | bytes 8388608 | tf_op jit(solution)/shard_map/clip_attention_backward/pallas_call | solution.py:394
  105.0 3.9 %lay_out.1 = (bf16[128,32,128]{2,1,0:T(8,128)(2,1)}, bf16[128,32,128]{2,1,0:T(8,128)(2,1)}, bf16[128,32,128]{2,1,0:T(8,128)(2,1)}, f32[1000,128]{1,0:T(8,128)}) custom-call(s32[16]{0:T(128)} %step_ref.3, f32[16,128]{1,0:T(8,128)} %get-tuple-element.10.total_ref, bf16[32,3,128,128]{3,2,1,0:T(8,128)(2,1)} %get-tuple-element.11.fin_hbm), custom_call_target="tpu_custom_call" | custom-call | flops 33554432 | bytes 7340032 | tf_op jit(solution)/shard_map/lay_out/pallas_call | solution.py:441

commit v3 on v2

--- a/solution.py
+++ b/solution.py
@@ -19,7 +19,9 @@
 STEPS = 1000
 QB = 256
 NEAR = 80.0
-AHEAD = 3
+AHEAD = 2
+FIRST = (0, 1, 2, 3, 5, 7)
+LATER = ((4, 0), (6, 2))
 LAG_COMPUTE = 3
 LAG_BACK = 7
 MESH = pl.DeviceIdType.MESH
@@ -232,11 +234,8 @@
         id_y(d).start()
     begin(jnp.int32(0))
 
-    def early(i, _):
-        zin_own(i).start()
-        return 0
-
-    lax.fori_loop(0, SLOTS, early, 0)
+    for i in FIRST:
+        zin_own(jnp.int32(i)).start()
     for i in range(1, AHEAD):
         begin(jnp.int32(i))
     gate_load.wait()
@@ -257,12 +256,17 @@
                 yin(t, d).wait_recv()
                 zin(t, lax.rem(y + NY - d, NY)).start()
             own_copy(t).wait()
+            for i, after in LATER:
+
+                @pl.when(t == after)
+                def _():
+                    zin_own(jnp.int32(i)).start()
 
             @pl.when(t + AHEAD < SLOTS)
             def _():
                 begin(t + AHEAD)
 
-        @pl.when(t == LAG_COMPUTE)
+        @pl.when(t == 1)
         def _():
             for n in range(2):
                 id_z(n).wait_recv()

time: 109 us -> 108 us (level)
  no operation moved by 1% of the time
where the time goes in v3:
time: 108 us
  Pallas kernels  107 us (99%)
    pallas_call x1, Pallas kernels, on_device(): pl.pallas_call(kernel, out_shape=(jax.ShapeDtypeStruct((HEADS, 3, BLK, HD...  103 us
    pallas_call x1, Pallas kernels, on_device(): pl.pallas_call(lay_out, out_shape=(grads, grads, grads, jax.ShapeDtypeStr...  3.87 us

profile of v3, /device:TPU:6, one launch (start us, length us, event | category | flops | bytes accessed | tf_op | source)
XLA Modules:
  0.0 107.8 jit_solution(9796777587225697855)
XLA Ops:
  0.6 103.3 %clip_attention_backward.1 = (bf16[32,3,128,128]{3,2,1,0:T(8,128)(2,1)}, f32[16,128]{1,0:T(8,128)}) custom-call(s32[16]{0:T(128)} %step_ref.3, f32[16]{0:T(128)} %weight_ref.1, bf16[128,32,128]{2,1,0:T(8,128)(2,1)} %q_hbm.1, bf16[128,32,128]{2,1,0:T(8,128)(2,1)} %k_hbm.1, bf16[128,32,128]{2,1,0:T(8,128)(2,1)} %v_hbm.1, bf16[128,32,128]{2,1,0:T(8,128)(2,1)} %c_hbm.1, ...), custom_call_target="tpu_custom_call" | custom-call | flops 12884901888 | bytes 8388608 | tf_op jit(solution)/shard_map/clip_attention_backward/pallas_call | solution.py:398
  103.9 3.9 %lay_out.1 = (bf16[128,32,128]{2,1,0:T(8,128)(2,1)}, bf16[128,32,128]{2,1,0:T(8,128)(2,1)}, bf16[128,32,128]{2,1,0:T(8,128)(2,1)}, f32[1000,128]{1,0:T(8,128)}) custom-call(s32[16]{0:T(128)} %step_ref.3, f32[16,128]{1,0:T(8,128)} %get-tuple-element.10.total_ref, bf16[32,3,128,128]{3,2,1,0:T(8,128)(2,1)} %get-tuple-element.11.fin_hbm), custom_call_target="tpu_custom_call" | custom-call | flops 33554432 | bytes 7340032 | tf_op jit(solution)/shard_map/lay_out/pallas_call | solution.py:445

commit v4 on v3

--- a/solution.py
+++ b/solution.py
@@ -23,7 +23,7 @@
 FIRST = (0, 1, 2, 3, 5, 7)
 LATER = ((4, 0), (6, 2))
 LAG_COMPUTE = 3
-LAG_BACK = 7
+LAG_BACK = 8
 MESH = pl.DeviceIdType.MESH
 F32 = jnp.float32
 BF16 = jnp.bfloat16

time: 108 us -> 117 us (1.083)
  Pallas kernels: 107 us -> 115 us
    pallas_call x1, Pallas kernels: 103 us -> 112 us  [on_device(): pl.pallas_call(kernel, out_shape=(jax.ShapeDtypeStruct((HEADS, 3, BLK, HD...]
where the time goes in v4:
time: 117 us; the launch traced here: 116 us
  Pallas kernels  115 us (98%)
    pallas_call x1, Pallas kernels, on_device(): pl.pallas_call(kernel, out_shape=(jax.ShapeDtypeStruct((HEADS, 3, BLK, HD...  112 us
    pallas_call x1, Pallas kernels, on_device(): pl.pallas_call(lay_out, out_shape=(grads, grads, grads, jax.ShapeDtypeStr...  3.87 us

profile of v4, /device:TPU:6, one launch (start us, length us, event | category | flops | bytes accessed | tf_op | source)
XLA Modules:
  0.0 116.1 jit_solution(11742130649533436752)
XLA Ops:
  0.6 111.6 %clip_attention_backward.1 = (bf16[32,3,128,128]{3,2,1,0:T(8,128)(2,1)}, f32[16,128]{1,0:T(8,128)}) custom-call(s32[16]{0:T(128)} %step_ref.3, f32[16]{0:T(128)} %weight_ref.1, bf16[128,32,128]{2,1,0:T(8,128)(2,1)} %q_hbm.1, bf16[128,32,128]{2,1,0:T(8,128)(2,1)} %k_hbm.1, bf16[128,32,128]{2,1,0:T(8,128)(2,1)} %v_hbm.1, bf16[128,32,128]{2,1,0:T(8,128)(2,1)} %c_hbm.1, ...), custom_call_target="tpu_custom_call" | custom-call | flops 12884901888 | bytes 8388608 | tf_op jit(solution)/shard_map/clip_attention_backward/pallas_call | solution.py:398
  112.3 3.9 %lay_out.1 = (bf16[128,32,128]{2,1,0:T(8,128)(2,1)}, bf16[128,32,128]{2,1,0:T(8,128)(2,1)}, bf16[128,32,128]{2,1,0:T(8,128)(2,1)}, f32[1000,128]{1,0:T(8,128)}) custom-call(s32[16]{0:T(128)} %step_ref.3, f32[16,128]{1,0:T(8,128)} %get-tuple-element.10.total_ref, bf16[32,3,128,128]{3,2,1,0:T(8,128)(2,1)} %get-tuple-element.11.fin_hbm), custom_call_target="tpu_custom_call" | custom-call | flops 33554432 | bytes 7340032 | tf_op jit(solution)/shard_map/lay_out/pallas_call | solution.py:445

commit v5 on v3

--- a/solution.py
+++ b/solution.py
@@ -294,12 +294,12 @@
             def _():
                 sum_in[z] = sum_out[i]
 
-        @pl.when((t >= LAG_BACK) & (lax.rem(t - LAG_BACK, 2) == 0))
+        @pl.when((t >= LAG_BACK) & (t != LAG_BACK + 2))
         def _():
             for d in (1, 2, 3, 0):
                 b = lax.rem(y + d, NY)
                 for odd in range(2):
-                    i = t - LAG_BACK + odd
+                    i = 2 * (t - LAG_BACK - jnp.where(t > LAG_BACK + 2, 1, 0)) + odd
                     zout(i, b).wait_recv()
                     theirs = idcol[part(ROW, b), :] == other_clip(idcol, odd)
                     for a in range(3):
@@ -315,7 +315,7 @@
 
         return 0
 
-    lax.fori_loop(0, SLOTS + LAG_BACK - 1, step, 0)
+    lax.fori_loop(0, LAG_BACK + SLOTS // 2 + 1, step, 0)
 
     def sums_arrived(i, _):
         @pl.when(i != z)

time: 108 us -> 112 us (1.037)
  Pallas kernels: 107 us -> 111 us
    pallas_call x1, Pallas kernels: 103 us -> 107 us  [on_device(): pl.pallas_call(kernel, out_shape=(jax.ShapeDtypeStruct((HEADS, 3, BLK, HD...]
where the time goes in v5:
time: 112 us; the launch traced here: 111 us
  Pallas kernels  111 us (99%)
    pallas_call x1, Pallas kernels, on_device(): pl.pallas_call(kernel, out_shape=(jax.ShapeDtypeStruct((HEADS, 3, BLK, HD...  107 us
    pallas_call x1, Pallas kernels, on_device(): pl.pallas_call(lay_out, out_shape=(grads, grads, grads, jax.ShapeDtypeStr...  3.87 us

profile of v5, /device:TPU:6, one launch (start us, length us, event | category | flops | bytes accessed | tf_op | source)
XLA Modules:
  0.0 111.4 jit_solution(7683683256480966124)
XLA Ops:
  0.6 106.9 %clip_attention_backward.1 = (bf16[32,3,128,128]{3,2,1,0:T(8,128)(2,1)}, f32[16,128]{1,0:T(8,128)}) custom-call(s32[16]{0:T(128)} %step_ref.3, f32[16]{0:T(128)} %weight_ref.1, bf16[128,32,128]{2,1,0:T(8,128)(2,1)} %q_hbm.1, bf16[128,32,128]{2,1,0:T(8,128)(2,1)} %k_hbm.1, bf16[128,32,128]{2,1,0:T(8,128)(2,1)} %v_hbm.1, bf16[128,32,128]{2,1,0:T(8,128)(2,1)} %c_hbm.1, ...), custom_call_target="tpu_custom_call" | custom-call | flops 12884901888 | bytes 8388608 | tf_op jit(solution)/shard_map/clip_attention_backward/pallas_call | solution.py:398
  107.5 3.9 %lay_out.1 = (bf16[128,32,128]{2,1,0:T(8,128)(2,1)}, bf16[128,32,128]{2,1,0:T(8,128)(2,1)}, bf16[128,32,128]{2,1,0:T(8,128)(2,1)}, f32[1000,128]{1,0:T(8,128)}) custom-call(s32[16]{0:T(128)} %step_ref.3, f32[16,128]{1,0:T(8,128)} %get-tuple-element.10.total_ref, bf16[32,3,128,128]{3,2,1,0:T(8,128)(2,1)} %get-tuple-element.11.fin_hbm), custom_call_target="tpu_custom_call" | custom-call | flops 33554432 | bytes 7340032 | tf_op jit(solution)/shard_map/lay_out/pallas_call | solution.py:445

commit v6 on v5

--- a/solution.py
+++ b/solution.py
@@ -23,7 +23,7 @@
 FIRST = (0, 1, 2, 3, 5, 7)
 LATER = ((4, 0), (6, 2))
 LAG_COMPUTE = 3
-LAG_BACK = 7
+LAG_BACK = 6
 MESH = pl.DeviceIdType.MESH
 F32 = jnp.float32
 BF16 = jnp.bfloat16
@@ -294,28 +294,35 @@
             def _():
                 sum_in[z] = sum_out[i]
 
-        @pl.when((t >= LAG_BACK) & (t != LAG_BACK + 2))
+        def take_back(i, d):
+            b = lax.rem(y + d, NY)
+            zout(i, b).wait_recv()
+            theirs = idcol[part(ROW, b), :] == other_clip(idcol, lax.rem(i, 2))
+            for a in range(3):
+                res[i, a, part(own_at(i), b), :] = jnp.where(
+                    theirs,
+                    back[i, a, part(0, b), :].astype(F32),
+                    res[i, a, part(own_at(i), b), :].astype(F32),
+                ).astype(BF16)
+            if d:
+                yout(i, d).start()
+            else:
+                fin_own(i).start()
+
+        @pl.when((t >= LAG_BACK) & (t < LAG_BACK + SLOTS // 2))
         def _():
             for d in (1, 2, 3, 0):
-                b = lax.rem(y + d, NY)
+                take_back(t - LAG_BACK, d)
+
+        @pl.when(t >= LAG_BACK + SLOTS // 2)
+        def _():
+            for d in (1, 2, 3, 0):
                 for odd in range(2):
-                    i = 2 * (t - LAG_BACK - jnp.where(t > LAG_BACK + 2, 1, 0)) + odd
-                    zout(i, b).wait_recv()
-                    theirs = idcol[part(ROW, b), :] == other_clip(idcol, odd)
-                    for a in range(3):
-                        res[i, a, part(ROW * odd, b), :] = jnp.where(
-                            theirs,
-                            back[i, a, part(0, b), :].astype(F32),
-                            res[i, a, part(ROW * odd, b), :].astype(F32),
-                        ).astype(BF16)
-                    if d:
-                        yout(i, d).start()
-                    else:
-                        fin_own(i).start()
+                    take_back(2 * (t - LAG_BACK) - SLOTS // 2 + odd, d)
 
         return 0
 
-    lax.fori_loop(0, LAG_BACK + SLOTS // 2 + 1, step, 0)
+    lax.fori_loop(0, LAG_BACK + SLOTS * 3 // 4, step, 0)
 
     def sums_arrived(i, _):
         @pl.when(i != z)

time: 112 us -> 108 us (0.964)
  Pallas kernels: 111 us -> 107 us
    pallas_call x1, Pallas kernels: 107 us -> 103 us  [on_device(): pl.pallas_call(kernel, out_shape=(jax.ShapeDtypeStruct((HEADS, 3, BLK, HD...]
where the time goes in v6:
time: 108 us
  Pallas kernels  107 us (99%)
    pallas_call x1, Pallas kernels, on_device(): pl.pallas_call(kernel, out_shape=(jax.ShapeDtypeStruct((HEADS, 3, BLK, HD...  103 us
    pallas_call x1, Pallas kernels, on_device(): pl.pallas_call(lay_out, out_shape=(grads, grads, grads, jax.ShapeDtypeStr...  3.87 us

profile of v6, /device:TPU:6, one launch (start us, length us, event | category | flops | bytes accessed | tf_op | source)
XLA Modules:
  0.0 107.7 jit_solution(6425422374920697788)
XLA Ops:
  0.6 103.1 %clip_attention_backward.1 = (bf16[32,3,128,128]{3,2,1,0:T(8,128)(2,1)}, f32[16,128]{1,0:T(8,128)}) custom-call(s32[16]{0:T(128)} %step_ref.3, f32[16]{0:T(128)} %weight_ref.1, bf16[128,32,128]{2,1,0:T(8,128)(2,1)} %q_hbm.1, bf16[128,32,128]{2,1,0:T(8,128)(2,1)} %k_hbm.1, bf16[128,32,128]{2,1,0:T(8,128)(2,1)} %v_hbm.1, bf16[128,32,128]{2,1,0:T(8,128)(2,1)} %c_hbm.1, ...), custom_call_target="tpu_custom_call" | custom-call | flops 12884901888 | bytes 8388608 | tf_op jit(solution)/shard_map/clip_attention_backward/pallas_call | solution.py:405
  103.8 3.9 %lay_out.1 = (bf16[128,32,128]{2,1,0:T(8,128)(2,1)}, bf16[128,32,128]{2,1,0:T(8,128)(2,1)}, bf16[128,32,128]{2,1,0:T(8,128)(2,1)}, f32[1000,128]{1,0:T(8,128)}) custom-call(s32[16]{0:T(128)} %step_ref.3, f32[16,128]{1,0:T(8,128)} %get-tuple-element.10.total_ref, bf16[32,3,128,128]{3,2,1,0:T(8,128)(2,1)} %get-tuple-element.11.fin_hbm), custom_call_target="tpu_custom_call" | custom-call | flops 33554432 | bytes 7340032 | tf_op jit(solution)/shard_map/lay_out/pallas_call | solution.py:452
